TPU v7x, 512 devices: a whole 4x4x16 slice. The times are simulated.
512 devices in a mesh: row: 64 (over z, y), grp: 8 (over x, core).
Axes of the slice: x: 4, y: 4, z: 16, core: 2. Of those that a mesh axis runs over, the one named last changes fastest.
Arguments:
- design: float32 [131072, 2048], P('row', 'grp')
- rademacher: int32 [131072], P('row'), may hold values from 0 to 1
- target: float32 [131072], P('row'), may hold values from -6 to 6
- sample_rows: int32 [64, 8, 16], P('row', 'grp'), may hold values from 0 to 2047
- checksum_seeds: int32 [2048], P('grp'), may hold values from 1 to 16
Outputs:
- solution: float32 [2048], P('grp')
- residual: float32 [131072], P('row')
- checksum: float32 [2048], P('grp')
Inputs may be any that keep to these rules, and one draw needn't show every extreme that they name: sample_rows holds row numbers within one index's block of 2048 rows; a row may be drawn more than once.
All inputs are finite; a program needn't handle non-finite values.
Results may differ from a plain program's by a relative error of at most 0.0003.
Values sent between devices are 32-bit elements; how exact they have to be, the bound alone decides.
No kernel may reach another device: no remote copies, remote signals or barrier semaphores. Data moves between devices by JAX's collectives and lax.ppermute only.
A program may use at most 64 MiB of HBM per device.

v0:
```python
import jax
import jax.numpy as jnp
from jax import lax
from jax.experimental import pallas as pl
from jax.experimental.pallas import tpu as pltpu
from jax.sharding import Mesh, PartitionSpec as P

Z, Y, X, C = 16, 4, 4, 2
ROWS = ("z", "y")
GRPS = ("x", "c")
F32 = jnp.float32
BF16 = jnp.bfloat16


def parity_sign(bits):
    bits = jnp.bitwise_xor(bits, jnp.right_shift(bits, 8))
    bits = jnp.bitwise_xor(bits, jnp.right_shift(bits, 4))
    odd = jnp.bitwise_and(jnp.right_shift(0x6996, jnp.bitwise_and(bits, 15)), 1)
    return 1.0 - 2.0 * odd.astype(F32)


def split3(value):
    hi = value.astype(BF16)
    rest = value - hi.astype(F32)
    mid = rest.astype(BF16)
    lo = (rest - mid.astype(F32)).astype(BF16)
    return hi, mid, lo


def sketch_kernel(pos_ref, idx_ref, rad_ref, tgt_ref, slab_ref, out_ref, sgn_ref, x_ref):
    count = idx_ref.shape[0]
    height, breadth = slab_ref.shape
    hi, mid, lo = split3(slab_ref[...])
    x_ref[0] = hi
    x_ref[1] = mid
    x_ref[2] = lo
    picks = jnp.broadcast_to(idx_ref[...], (count, 128))
    lane = lax.broadcasted_iota(jnp.int32, (count, 128), 1)
    slot = lax.broadcasted_iota(jnp.int32, (count, 128), 0)
    far = parity_sign(jnp.bitwise_and(jnp.right_shift(slot, 4), pos_ref[0]))
    base = parity_sign(jnp.bitwise_and(picks, lane)) * far * 0.03125
    base = base.astype(BF16)
    flips = [
        (1.0 - 2.0 * jnp.bitwise_and(jnp.right_shift(picks, 7 + b), 1).astype(F32)).astype(BF16)
        for b in range(4)
    ]
    row_sign = (1.0 - 2.0 * rad_ref[...].astype(F32)).astype(BF16)
    gray = 0
    current = base
    for step in range(height // 128):
        new = step ^ (step >> 1)
        if step:
            current = current * flips[(new ^ gray).bit_length() - 1]
        gray = new
        sgn_ref[0:count, gray * 128 : (gray + 1) * 128] = (
            current * row_sign[:, gray * 128 : (gray + 1) * 128]
        )
    thi, tmid, tlo = split3(tgt_ref[...])
    sgn_ref[count : count + 16, :] = jnp.concatenate(
        [thi, tmid, tlo, jnp.zeros((13, height), BF16)], axis=0
    )

    def product(rows):
        total = jnp.dot(rows, x_ref[0], preferred_element_type=F32)
        total += jnp.dot(rows, x_ref[1], preferred_element_type=F32)
        return total + jnp.dot(rows, x_ref[2], preferred_element_type=F32)

    back = jnp.sum(product(sgn_ref[count : count + 16, :]), axis=0, keepdims=True)
    for part in range(Y):
        out_ref[part, 0:256, :] = product(sgn_ref[part * 256 : (part + 1) * 256, :])
        out_ref[part, 256:264, :] = jnp.broadcast_to(back, (8, breadth))


def sketch(position, picks, rademacher, target, design):
    height, breadth = design.shape
    vmem = pl.BlockSpec(memory_space=pltpu.VMEM)
    return pl.pallas_call(
        sketch_kernel,
        out_shape=jax.ShapeDtypeStruct((Y, 264, breadth), F32),
        in_specs=[pl.BlockSpec(memory_space=pltpu.SMEM), vmem, vmem, vmem, vmem],
        out_specs=vmem,
        scratch_shapes=[
            pltpu.VMEM((1024 + 16, height), BF16),
            pltpu.VMEM((3, height, breadth), BF16),
        ],
        compiler_params=pltpu.CompilerParams(vmem_limit_bytes=40 * 2**20),
        name="sketch",
    )(position, picks, rademacher, target, design)


def exchange(pieces, axes):
    return lax.all_to_all(pieces, axes, split_axis=0, concat_axis=0, tiled=True)


def share(value, axes, count):
    return exchange(jnp.broadcast_to(value[None], (count,) + value.shape), axes)


NB = 16


def row_bcast(value, row):
    return jnp.broadcast_to(value[row : row + 1, :], value.shape)


def dot_nt(left, right):
    return lax.dot_general(left, right, (((1,), (1,)), ((), ())), preferred_element_type=F32)


def dot_tn(left, right):
    return lax.dot_general(left, right, (((0,), (0,)), ((), ())), preferred_element_type=F32)


def factor_kernel(gram_ref, back_ref, seed_ref, slab_ref, image_ref, dir_ref, check_ref, work_ref):
    size = gram_ref.shape[1]
    height = slab_ref.shape[0]
    gram = gram_ref[0]
    for part in range(1, gram_ref.shape[0]):
        gram = gram + gram_ref[part]
    sub = lax.broadcasted_iota(jnp.int32, (128, size), 0)
    weights = seed_ref[...].astype(F32) * 0.0625
    weight_rows = jnp.where(sub == 1, jnp.broadcast_to(weights, (128, size)), 0.0).astype(BF16)
    back_rows = jnp.where(sub == 0, jnp.broadcast_to(back_ref[...], (128, size)), 0.0)
    eye = (
        lax.broadcasted_iota(jnp.int32, (size, size), 0)
        == lax.broadcasted_iota(jnp.int32, (size, size), 1)
    ).astype(BF16)
    extra = jnp.zeros((size, 128), F32)
    for term in split3(gram):
        extra = extra + dot_nt(term, weight_rows)
    for term in split3(back_rows):
        extra = extra + dot_nt(eye, term)
    work_ref[:, :size] = gram
    work_ref[:, size:] = extra

    wide = size + 128
    lane = lax.broadcasted_iota(jnp.int32, (NB, wide), 1)
    row = lax.broadcasted_iota(jnp.int32, (NB, wide), 0)
    small_row = lax.broadcasted_iota(jnp.int32, (NB, 128), 0)
    for block in range(size // NB):
        at = block * NB
        panel = work_ref[at : at + NB, :]
        cols = [jnp.broadcast_to(panel[:, at + j : at + j + 1], (NB, 128)) for j in range(NB)]
        panel = jnp.where((lane >= at) & (lane < at + NB), (lane - at == row).astype(F32), panel)
        scale = jnp.zeros((NB, 128), F32)
        for j in range(NB):
            pivot = row_bcast(cols[j], j)
            coef = jnp.where(small_row > j, cols[j] / pivot, 0.0)
            scale = jnp.where(small_row == j, pivot, scale)
            for later in range(j + 1, NB):
                cols[later] = cols[later] - coef * row_bcast(cols[later], j)
            panel = panel - jnp.tile(coef, (1, wide // 128)) * row_bcast(panel, j)
        panel = panel * jnp.tile(lax.rsqrt(scale), (1, wide // 128))
        work_ref[at : at + NB, :] = panel
        if at + NB < size:
            hi, mid, lo = split3(panel)
            zero = jnp.zeros((NB, size), BF16)
            keep = lane[:, :size] >= at + NB
            lhi, lmid, llo = [jnp.where(keep, term[:, :size], zero) for term in (hi, mid, lo)]
            left = jnp.concatenate([lhi, lhi, lmid, lhi, llo, lmid], axis=0)
            right = jnp.concatenate([hi, mid, hi, lo, hi, mid], axis=0)
            change = dot_tn(left, right)
            rest = size - at - NB
            wide_lane = lax.broadcasted_iota(jnp.int32, (rest, wide), 1)
            old = work_ref[at + NB :, :]
            old = jnp.where((wide_lane >= at) & (wide_lane < at + NB), 0.0, old)
            work_ref[at + NB :, :] = old - change[at + NB :, :]

    lower_inv = jnp.where(
        lax.broadcasted_iota(jnp.int32, (size, size), 0)
        >= lax.broadcasted_iota(jnp.int32, (size, size), 1),
        work_ref[:, :size],
        0.0,
    )
    half = work_ref[:, size : size + 1]
    check = work_ref[:, size + 1 : size + 2]
    direction = jnp.sum(lower_inv * half, axis=0, keepdims=True)
    diagonal = eye.astype(F32)
    check_ref[...] = jnp.sum(diagonal * check, axis=0, keepdims=True)
    dir_ref[...] = direction
    energy = jnp.sum(half * half, axis=0, keepdims=True)

    dhi, dmid, dlo = split3(direction)
    rows = jnp.concatenate([dhi, dmid, dlo, jnp.zeros((13, size), BF16)], axis=0)
    for part in range(height // 256):
        total = jnp.zeros((16, 256), F32)
        for term in split3(slab_ref[part * 256 : (part + 1) * 256, :]):
            total = total + dot_nt(rows, term)
        image = jnp.sum(total, axis=0, keepdims=True)
        image_ref[:, part * 256 : (part + 1) * 256] = jnp.broadcast_to(image, (8, 256))
    image_ref[:, height:] = jnp.broadcast_to(energy, (8, 128))


def factor(grams, back, seeds, design):
    height, breadth = design.shape
    vmem = pl.BlockSpec(memory_space=pltpu.VMEM)
    return pl.pallas_call(
        factor_kernel,
        out_shape=(
            jax.ShapeDtypeStruct((8, height + 128), F32),
            jax.ShapeDtypeStruct((1, breadth), F32),
            jax.ShapeDtypeStruct((1, breadth), F32),
        ),
        in_specs=[vmem] * 4,
        out_specs=(vmem, vmem, vmem),
        scratch_shapes=[pltpu.VMEM((breadth, breadth + 128), F32)],
        compiler_params=pltpu.CompilerParams(vmem_limit_bytes=40 * 2**20),
        name="factor",
    )(grams, back, seeds, design)


def body(design, rademacher, target, sample_rows, checksum_seeds):
    highest = lax.Precision.HIGHEST
    height, breadth = design.shape
    position = lax.axis_index(ROWS).astype(jnp.int32).reshape(1)
    picks = share(sample_rows.reshape(16), "y", Y).reshape(Y * 16)
    picks = share(picks, "z", Z).reshape(Z * Y * 16, 1)
    parts = sketch(
        position, picks, rademacher.reshape(1, height), target.reshape(1, height), design
    )
    mine = jnp.sum(exchange(parts, "y"), axis=0)
    pieces = jnp.concatenate(
        [mine[:256].reshape(Z, 16, breadth), jnp.broadcast_to(mine[None, 256:], (Z, 8, breadth))],
        axis=1,
    )
    mine = jnp.sum(exchange(pieces, "z"), axis=0)
    rows = lax.all_gather(mine[:16], "z", axis=0, tiled=True)
    gram = jnp.dot(rows.T, rows, precision=highest, preferred_element_type=F32)
    grams = share(gram, "y", Y)
    images, direction, checksum = factor(
        grams, mine[16:17], checksum_seeds.reshape(1, breadth), design
    )
    packed = jnp.sum(exchange(images, GRPS), axis=0)
    image = packed[:height]
    numer = packed[height]
    near = lax.psum(jnp.sum(image * image), "y")
    denom = jnp.sum(share(jnp.broadcast_to(near, (1, 128)), "z", Z), axis=(0, 1))[0]
    step = numer / denom
    return (
        step * direction.reshape(breadth),
        target - step * image,
        checksum.reshape(breadth),
    )


def solution(mesh):
    fine = Mesh(mesh.devices.reshape(Z, Y, X, C), ROWS + GRPS)
    in_specs = (P(ROWS, GRPS), P(ROWS), P(ROWS), P(ROWS, GRPS, None), P(GRPS))
    out_specs = (P(GRPS), P(ROWS), P(GRPS))
    return jax.shard_map(body, mesh=fine, in_specs=in_specs, out_specs=out_specs, check_vma=False)
```

profile of v0, /device:TPU:1, one launch (start us, length us, event | category | flops | bytes accessed | tf_op | source)
XLA Modules:
  0.0 181.5 jit_solution(8543651743774425575)
XLA Ops:
  0.6 0.7 broadcast_in_dim.10
  1.3 8.9 %all_to_all.41 = s32[4,1,16]{2,1,0:T(1,128)S(1)} all-to-all(s32[4,1,16]{2,1,0:T(1,128)S(1)} %broadcast_in_dim.10), channel_id=1, replica_groups=mesh['z'=16,'y'=4,'x'=4,'c'=2] {'y'}, dimensions={0} | all-to-all | bytes 512 | tf_op jit(solution)/shard_map/all_to_all | solution.py:92
  10.7 0.7 reduce.7
  11.5 0.6 broadcast_in_dim.12
  12.1 14.9 %all-to-all-start.1 = ((s32[16,1,64]{2,1,0:T(1,128)}), s32[16,1,64]{2,1,0:T(1,128)S(1)}, u32[]{:S(2)}, u32[]{:S(2)}) async-start(s32[16,1,64]{2,1,0:T(1,128)} %broadcast_in_dim.12), calls=%async_computation.1 | async-start | bytes 16384 | tf_op jit(solution)/shard_map/all_to_all | solution.py:92
  27.0 11.2 %all-to-all-done.1 = s32[16,1,64]{2,1,0:T(1,128)S(1)} async-done(((s32[16,1,64]{2,1,0:T(1,128)}), s32[16,1,64]{2,1,0:T(1,128)S(1)}, u32[]{:S(2)}, u32[]{:S(2)}) %all-to-all-start.1) | async-done | bytes 4128 | tf_op jit(solution)/shard_map/all_to_all | solution.py:92
  38.2 0.7 reduce.8
  39.4 1.6 copy-done
  41.0 0.7 copy-done.2
  41.7 0.7 copy-done.4
  42.4 5.3 %sketch.1 = f32[4,264,256]{2,1,0:T(8,128)S(1)} custom-call(s32[1]{0:T(128)} %bitcast.pos_ref, s32[1024,1]{1,0:T(8,128)S(1)} %reshape.59.idx_ref, s32[1,2048]{1,0:T(1,128)S(1)} %bitcast.16, f32[1,2048]{1,0:T(1,128)S(1)} %bitcast.15, f32[2048,256]{1,0:T(8,128)S(1)} %copy-done), custom_call_target="tpu_custom_call" | custom-call | tf_op jit(solution)/shard_map/sketch/pallas_call | solution.py:77
  47.7 14.0 %all_to_all.42 = f32[4,264,256]{2,1,0:T(8,128)S(1)} all-to-all(f32[4,264,256]{2,1,0:T(8,128)S(1)} %sketch.1), channel_id=1, replica_groups=mesh['z'=16,'y'=4,'x'=4,'c'=2] {'y'}, dimensions={0} | all-to-all | bytes 2162688 | tf_op jit(solution)/shard_map/all_to_all | solution.py:92
  61.9 17.3 %all_to_all.43 = f32[16,24,256]{2,1,0:T(8,128)S(1)} all-to-all(f32[16,24,256]{2,1,0:T(8,128)S(1)} %pad_maximum_fusion), channel_id=1, replica_groups=mesh['z'=16,'y'=4,'x'=4,'c'=2] {'z'}, dimensions={0} | all-to-all | bytes 786432 | tf_op jit(solution)/shard_map/all_to_all | solution.py:92
  79.2 26.4 %all_gather.3 = f32[256,256]{1,0:T(8,128)S(1)} all-gather(f32[16,256]{1,0:T(8,128)S(1)} %slice.30), channel_id=1, replica_groups=mesh['z'=16,'y'=4,'x'=4,'c'=2] {'z'}, dimensions={0}, use_global_device_ids=true | all-gather | bytes 278528 | tf_op jit(solution)/shard_map/all_gather | solution.py:227
  106.2 1.1 broadcast_in_dim.28
  107.3 3.8 %all-to-all-start.4 = ((f32[4,256,256]{2,1,0:T(8,128)}), f32[4,256,256]{2,1,0:T(8,128)S(1)}, u32[]{:S(2)}, u32[]{:S(2)}) async-start(f32[4,256,256]{2,1,0:T(8,128)} %broadcast_in_dim.28), calls=%async_computation.4 | async-start | bytes 2097152 | tf_op jit(solution)/shard_map/all_to_all | solution.py:92
  111.2 9.5 %all-to-all-done.4.gram_ref = f32[4,256,256]{2,1,0:T(8,128)S(1)} async-done(((f32[4,256,256]{2,1,0:T(8,128)}), f32[4,256,256]{2,1,0:T(8,128)S(1)}, u32[]{:S(2)}, u32[]{:S(2)}) %all-to-all-start.4) | async-done | bytes 1048608 | tf_op jit(solution)/shard_map/all_to_all | solution.py:92
  120.7 8.8 %factor.1 = (f32[8,2176]{1,0:T(8,128)S(1)}, f32[1,256]{1,0:T(1,128)S(1)}, f32[1,256]{1,0:T(1,128)}) custom-call(f32[4,256,256]{2,1,0:T(8,128)S(1)} %all-to-all-done.4.gram_ref, f32[1,256]{1,0:T(1,128)S(1)} %slice.31.back_ref, s32[1,256]{1,0:T(1,128)S(1)} %bitcast.17, f32[2048,256]{1,0:T(8,128)S(1)} %copy-done.1), custom_call_target="tpu_custom_call" | custom-call | tf_op jit(solution)/shard_map/factor/pallas_call | solution.py:197
  129.6 24.6 %all_to_all.44 = f32[8,1,2176]{2,1,0:T(1,128)S(1)} all-to-all(f32[8,1,2176]{2,1,0:T(1,128)S(1)} %copy.14), channel_id=1, replica_groups=mesh['z'=16,'y'=4,'x'=4,'c'=2] {'x','c'}, dimensions={0} | all-to-all | bytes 139264 | tf_op jit(solution)/shard_map/all_to_all | solution.py:92
  154.8 7.5 %psum.7 = f32[]{:T(128)} all-reduce(f32[]{:T(128)} %multiply_reduce_fusion), channel_id=1, replica_groups=mesh['z'=16,'y'=4,'x'=4,'c'=2] {'y'}, use_global_device_ids=true, to_apply=%region_4.0 | all-reduce | flops 1 | bytes 8 | tf_op jit(solution)/shard_map/psum | solution.py:236
  162.3 1.2 broadcast_in_dim_broadcast_in_dim_broadcast_in_dim.3
  163.6 4.8 %all-to-all-start.6 = ((f32[16,1,128]{2,1,0:T(1,128)}), f32[16,1,128]{2,1,0:T(1,128)S(1)}, u32[]{:S(2)}, u32[]{:S(2)}) async-start(f32[16,1,128]{2,1,0:T(1,128)} %broadcast_in_dim_broadcast_in_dim_broadcast_in_dim.3), calls=%async_computation.6 | async-start | bytes 16384 | tf_op jit(solution)/shard_map/all_to_all | solution.py:92
  168.9 10.7 %all-to-all-done.6 = f32[16,1,128]{2,1,0:T(1,128)S(1)} async-done(((f32[16,1,128]{2,1,0:T(1,128)}), f32[16,1,128]{2,1,0:T(1,128)S(1)}, u32[]{:S(2)}, u32[]{:S(2)}) %all-to-all-start.6) | async-done | bytes 8224 | tf_op jit(solution)/shard_map/all_to_all | solution.py:92
  180.3 0.6 multiply_subtract_fusion
  (27 shorter events, 3.7 us)
Async XLA Ops:
  12.1 26.1 %all-to-all-start.1 = ((s32[16,1,64]{2,1,0:T(1,128)}), s32[16,1,64]{2,1,0:T(1,128)S(1)}, u32[]{:S(2)}, u32[]{:S(2)}) async-start(s32[16,1,64]{2,1,0:T(1,128)} %broadcast_in_dim.12), calls=%async_computation.1 | async-start | bytes 16384 | tf_op jit(solution)/shard_map/all_to_all | solution.py:92
  39.4 1.6 copy-start
  41.0 0.7 copy-start.2
  41.7 0.7 copy-start.4
  107.3 13.4 %copy-start.1 = (f32[2048,256]{1,0:T(8,128)S(1)}, f32[2048,256]{1,0:T(8,128)}, u32[]{:S(2)}) copy-start(f32[2048,256]{1,0:T(8,128)} %slab_ref.3) | copy-start | bytes 6291460
  107.3 13.4 %copy-start.5 = (s32[256]{0:T(256)S(1)}, s32[256]{0:T(256)}, u32[]{:S(2)}) copy-start(s32[256]{0:T(256)} %param.9) | copy-start | bytes 3076
  107.3 13.4 %all-to-all-start.4 = ((f32[4,256,256]{2,1,0:T(8,128)}), f32[4,256,256]{2,1,0:T(8,128)S(1)}, u32[]{:S(2)}, u32[]{:S(2)}) async-start(f32[4,256,256]{2,1,0:T(8,128)} %broadcast_in_dim.28), calls=%async_computation.4 | async-start | bytes 2097152 | tf_op jit(solution)/shard_map/all_to_all | solution.py:92
  120.7 59.7 %copy-start.3 = (f32[2048]{0:T(1024)S(1)}, f32[2048]{0:T(1024)}, u32[]{:S(2)}) copy-start(f32[2048]{0:T(1024)} %param.7) | copy-start | bytes 24580
  163.6 16.1 %all-to-all-start.6 = ((f32[16,1,128]{2,1,0:T(1,128)}), f32[16,1,128]{2,1,0:T(1,128)S(1)}, u32[]{:S(2)}, u32[]{:S(2)}) async-start(f32[16,1,128]{2,1,0:T(1,128)} %broadcast_in_dim_broadcast_in_dim_broadcast_in_dim.3), calls=%async_computation.6 | async-start | bytes 16384 | tf_op jit(solution)/shard_map/all_to_all | solution.py:92
where the time goes:
time: 184 us; the launch traced here: 182 us
  blocking collectives  98.7 us (54%)
  waiting for transfers between devices  31.4 us (17%)
  starting transfers between devices  23.6 us (13%)
  Pallas kernels  14.1 us (8%)
  local copies, waits for them, and re-layouts  8.26 us (4%)
  other arithmetic  3.31 us (2%)
    all_to_all x4, blocking collectives, exchange(): return lax.all_to_all(pieces, axes, split_axis=0, concat_axis=0, tiled=True)  64.8 us
    all_to_all x3, waiting for transfers between devices, exchange(): return lax.all_to_all(pieces, axes, split_axis=0, concat_axis=0, tiled=True)  31.4 us
    all_gather x1, blocking collectives, body(): rows = lax.all_gather(mine[:16], 'z', axis=0, tiled=True)  26.4 us
    all_to_all x3, starting transfers between devices, exchange(): return lax.all_to_all(pieces, axes, split_axis=0, concat_axis=0, tiled=True)  23.6 us
    pallas_call x1, Pallas kernels, factor(): pl.pallas_call(factor_kernel, out_shape=(jax.ShapeDtypeStruct((8, height...  8.8 us
    psum x1, blocking collectives, body(): near = lax.psum(jnp.sum(image * image), 'y')  7.48 us
    pallas_call x1, Pallas kernels, sketch(): pl.pallas_call(sketch_kernel, out_shape=jax.ShapeDtypeStruct((Y, 264, bre...  5.34 us
  transfers between devices with their start and end apart: 3, of which 3 were waited for; matrix products, arithmetic and copies ran while one was open for 0% of the time, Pallas kernels for 0%

commit v1 on v0

--- a/solution.py
+++ b/solution.py
@@ -27,7 +27,8 @@
     return hi, mid, lo
 
 
-def sketch_kernel(pos_ref, idx_ref, rad_ref, tgt_ref, slab_ref, out_ref, sgn_ref, x_ref):
+def sketch_kernel(pos_ref, idx_ref, rad_ref, tgt_ref, slab_ref, *refs):
+    out_refs, (sgn_ref, x_ref) = refs[:Y], refs[Y:]
     count = idx_ref.shape[0]
     height, breadth = slab_ref.shape
     hi, mid, lo = split3(slab_ref[...])
@@ -37,7 +38,15 @@
     picks = jnp.broadcast_to(idx_ref[...], (count, 128))
     lane = lax.broadcasted_iota(jnp.int32, (count, 128), 1)
     slot = lax.broadcasted_iota(jnp.int32, (count, 128), 0)
-    far = parity_sign(jnp.bitwise_and(jnp.right_shift(slot, 4), pos_ref[0]))
+    place = jnp.right_shift(slot, 4)
+    origin = jnp.bitwise_or(
+        jnp.bitwise_or(
+            jnp.left_shift(jnp.bitwise_and(place, 3), 4), jnp.bitwise_and(place, 12)
+        ),
+        jnp.right_shift(place, 4),
+    )
+    origin = jnp.bitwise_xor(origin, pos_ref[0])
+    far = parity_sign(jnp.bitwise_and(origin, pos_ref[0]))
     base = parity_sign(jnp.bitwise_and(picks, lane)) * far * 0.03125
     base = base.astype(BF16)
     flips = [
@@ -66,9 +75,9 @@
         return total + jnp.dot(rows, x_ref[2], preferred_element_type=F32)
 
     back = jnp.sum(product(sgn_ref[count : count + 16, :]), axis=0, keepdims=True)
-    for part in range(Y):
-        out_ref[part, 0:256, :] = product(sgn_ref[part * 256 : (part + 1) * 256, :])
-        out_ref[part, 256:264, :] = jnp.broadcast_to(back, (8, breadth))
+    for part, out_ref in enumerate(out_refs):
+        out_ref[0:256, :] = product(sgn_ref[part * 256 : (part + 1) * 256, :])
+        out_ref[256:264, :] = jnp.broadcast_to(back, (8, breadth))
 
 
 def sketch(position, picks, rademacher, target, design):
@@ -76,9 +85,9 @@
     vmem = pl.BlockSpec(memory_space=pltpu.VMEM)
     return pl.pallas_call(
         sketch_kernel,
-        out_shape=jax.ShapeDtypeStruct((Y, 264, breadth), F32),
+        out_shape=[jax.ShapeDtypeStruct((264, breadth), F32)] * Y,
         in_specs=[pl.BlockSpec(memory_space=pltpu.SMEM), vmem, vmem, vmem, vmem],
-        out_specs=vmem,
+        out_specs=[vmem] * Y,
         scratch_shapes=[
             pltpu.VMEM((1024 + 16, height), BF16),
             pltpu.VMEM((3, height, breadth), BF16),
@@ -92,8 +101,17 @@
     return lax.all_to_all(pieces, axes, split_axis=0, concat_axis=0, tiled=True)
 
 
-def share(value, axes, count):
-    return exchange(jnp.broadcast_to(value[None], (count,) + value.shape), axes)
+def swap(value, axis, mask):
+    pairs = [(source, source ^ mask) for source in range(lax.axis_size(axis))]
+    return lax.ppermute(value, axis, pairs)
+
+
+def fan(pieces, axis, stride):
+    return [pieces[0]] + [swap(pieces[j], axis, j * stride) for j in range(1, 4)]
+
+
+def total(pieces):
+    return (pieces[0] + pieces[1]) + (pieces[2] + pieces[3])
 
 
 NB = 16
@@ -111,12 +129,41 @@
     return lax.dot_general(left, right, (((0,), (0,)), ((), ())), preferred_element_type=F32)
 
 
-def factor_kernel(gram_ref, back_ref, seed_ref, slab_ref, image_ref, dir_ref, check_ref, work_ref):
-    size = gram_ref.shape[1]
+def gram_kernel(row0, row1, row2, row3, out_ref):
+    rows = jnp.concatenate([row0[...], row1[...], row2[...], row3[...]], axis=0)
+    hi, mid, lo = split3(rows)
+    left = jnp.concatenate([hi, hi, mid, hi, lo, mid], axis=0)
+    right = jnp.concatenate([hi, mid, hi, lo, hi, mid], axis=0)
+    out_ref[0:128, :] = dot_tn(left[:, :128], right[:, :128])
+    out_ref[128:256, :] = dot_tn(left[:, :128], right[:, 128:])
+    out_ref[256:384, :] = dot_tn(left[:, 128:], right[:, 128:])
+
+
+def gram_blocks(rows):
+    vmem = pl.BlockSpec(memory_space=pltpu.VMEM)
+    return pl.pallas_call(
+        gram_kernel,
+        out_shape=jax.ShapeDtypeStruct((384, 128), F32),
+        in_specs=[vmem] * 4,
+        out_specs=vmem,
+        name="gram",
+    )(*rows)
+
+
+def factor_kernel(
+    gram0, gram1, gram2, gram3, back_ref, seed_ref, slab_ref, image_ref, dir_ref, check_ref, work_ref
+):
+    size = slab_ref.shape[1]
     height = slab_ref.shape[0]
-    gram = gram_ref[0]
-    for part in range(1, gram_ref.shape[0]):
-        gram = gram + gram_ref[part]
+    blocks = (gram0[...] + gram1[...]) + (gram2[...] + gram3[...])
+    corner = blocks[128:256]
+    gram = jnp.concatenate(
+        [
+            jnp.concatenate([blocks[0:128], corner], axis=1),
+            jnp.concatenate([corner.T, blocks[256:384]], axis=1),
+        ],
+        axis=0,
+    )
     sub = lax.broadcasted_iota(jnp.int32, (128, size), 0)
     weights = seed_ref[...].astype(F32) * 0.0625
     weight_rows = jnp.where(sub == 1, jnp.broadcast_to(weights, (128, size)), 0.0).astype(BF16)
@@ -201,41 +248,44 @@
             jax.ShapeDtypeStruct((1, breadth), F32),
             jax.ShapeDtypeStruct((1, breadth), F32),
         ),
-        in_specs=[vmem] * 4,
+        in_specs=[vmem] * 7,
         out_specs=(vmem, vmem, vmem),
         scratch_shapes=[pltpu.VMEM((breadth, breadth + 128), F32)],
         compiler_params=pltpu.CompilerParams(vmem_limit_bytes=40 * 2**20),
         name="factor",
-    )(grams, back, seeds, design)
+    )(*grams, back, seeds, design)
 
 
 def body(design, rademacher, target, sample_rows, checksum_seeds):
-    highest = lax.Precision.HIGHEST
     height, breadth = design.shape
     position = lax.axis_index(ROWS).astype(jnp.int32).reshape(1)
-    picks = share(sample_rows.reshape(16), "y", Y).reshape(Y * 16)
-    picks = share(picks, "z", Z).reshape(Z * Y * 16, 1)
+    picks = sample_rows.reshape(1, 16)
+    for axis, mask in (("z", 4), ("z", 8), ("z", 1), ("z", 2), ("y", 1), ("y", 2)):
+        picks = jnp.concatenate([picks, swap(picks, axis, mask)], axis=0)
     parts = sketch(
-        position, picks, rademacher.reshape(1, height), target.reshape(1, height), design
-    )
-    mine = jnp.sum(exchange(parts, "y"), axis=0)
-    pieces = jnp.concatenate(
-        [mine[:256].reshape(Z, 16, breadth), jnp.broadcast_to(mine[None, 256:], (Z, 8, breadth))],
-        axis=1,
-    )
-    mine = jnp.sum(exchange(pieces, "z"), axis=0)
-    rows = lax.all_gather(mine[:16], "z", axis=0, tiled=True)
-    gram = jnp.dot(rows.T, rows, precision=highest, preferred_element_type=F32)
-    grams = share(gram, "y", Y)
+        position,
+        picks.reshape(Z * Y * 16, 1),
+        rademacher.reshape(1, height),
+        target.reshape(1, height),
+        design,
+    )
+    mine = total(fan(parts, "y", 1))
+    pieces = [jnp.concatenate([mine[64 * j : 64 * j + 64], mine[256:]]) for j in range(4)]
+    mine = total(fan(pieces, "z", 1))
+    pieces = [jnp.concatenate([mine[16 * j : 16 * j + 16], mine[64:]]) for j in range(4)]
+    mine = total(fan(pieces, "z", 4))
+    rows = jnp.concatenate(fan([mine[:16]] * 4, "z", 4))
+    blocks = gram_blocks(fan([rows] * 4, "z", 1))
     images, direction, checksum = factor(
-        grams, mine[16:17], checksum_seeds.reshape(1, breadth), design
+        fan([blocks] * 4, "y", 1), mine[16:17], checksum_seeds.reshape(1, breadth), design
     )
     packed = jnp.sum(exchange(images, GRPS), axis=0)
     image = packed[:height]
     numer = packed[height]
-    near = lax.psum(jnp.sum(image * image), "y")
-    denom = jnp.sum(share(jnp.broadcast_to(near, (1, 128)), "z", Z), axis=(0, 1))[0]
-    step = numer / denom
+    denom = jnp.broadcast_to(jnp.sum(image * image), (1, 128))
+    for axis, stride in (("y", 1), ("z", 1), ("z", 4)):
+        denom = total(fan([denom] * 4, axis, stride))
+    step = numer / denom[0, 0]
     return (
         step * direction.reshape(breadth),
         target - step * image,

time: 184 us -> 247 us (1.34)
  starting transfers between devices: 23.6 us -> 143 us
  blocking collectives: 98.7 us -> 26.1 us
  waiting for transfers between devices: 31.4 us -> 41.7 us
    ppermute x0 -> x33, starting transfers between devices: none -> 143 us  [swap(): return lax.ppermute(value, axis, pairs)]
    ppermute x0 -> x33, waiting for transfers between devices: none -> 41.7 us  [swap(): return lax.ppermute(value, axis, pairs)]
    all_to_all x4 -> x1, blocking collectives: 64.8 us -> 26.1 us  [exchange(): return lax.all_to_all(pieces, axes, split_axis=0, concat_axis=0, tiled=True)]
    all_to_all x3 -> x0, waiting for transfers between devices: 31.4 us -> none  [exchange(): return lax.all_to_all(pieces, axes, split_axis=0, concat_axis=0, tiled=True)]
    all_gather x1 -> x0, blocking collectives: 26.4 us -> none  [body(): rows = lax.all_gather(mine[:16], 'z', axis=0, tiled=True)]
    all_to_all x3 -> x0, starting transfers between devices: 23.6 us -> none  [exchange(): return lax.all_to_all(pieces, axes, split_axis=0, concat_axis=0, tiled=True)]
    psum x1 -> x0, blocking collectives: 7.48 us -> none  [body(): near = lax.psum(jnp.sum(image * image), 'y')]
    pallas_call x1 -> x2, Pallas kernels: 5.34 us -> 7.58 us  [the longest x1 5.46 us: sketch(): pl.pallas_call(sketch_kernel, out_shape=[jax.ShapeDtypeStruct((264, bread...]
  transfers between devices with their start and end apart: 3 -> 33, of which waited for: 3 -> 19; matrix products, arithmetic and copies ran while one was open for 0% -> 0% of each run, Pallas kernels for 0% -> 0%
where the time goes in v1:
time: 247 us; the launch traced here: 242 us
  starting transfers between devices  143 us (58%)
  waiting for transfers between devices  41.7 us (17%)
  blocking collectives  26.1 us (11%)
  Pallas kernels  16.4 us (7%)
  local copies, waits for them, and re-layouts  8.15 us (3%)
  other arithmetic  4.6 us (2%)
    ppermute x33, starting transfers between devices, swap(): return lax.ppermute(value, axis, pairs)  143 us
    ppermute x33, waiting for transfers between devices, swap(): return lax.ppermute(value, axis, pairs)  41.7 us
    all_to_all x1, blocking collectives, exchange(): return lax.all_to_all(pieces, axes, split_axis=0, concat_axis=0, tiled=True)  26.1 us
    pallas_call x1, Pallas kernels, factor(): pl.pallas_call(factor_kernel, out_shape=(jax.ShapeDtypeStruct((8, height...  8.78 us
    pallas_call x1, Pallas kernels, sketch(): pl.pallas_call(sketch_kernel, out_shape=[jax.ShapeDtypeStruct((264, bread...  5.46 us
  transfers between devices with their start and end apart: 33, of which 19 were waited for; matrix products, arithmetic and copies ran while one was open for 0% of the time, Pallas kernels for 0%

profile of v1, /device:TPU:1, one launch (start us, length us, event | category | flops | bytes accessed | tf_op | source)
XLA Modules:
  0.0 242.2 jit_solution(6251848269087519987)
XLA Ops:
  0.6 9.6 %collective-permute-start = (s32[1,16]{1,0:T(1,128)}, s32[1,16]{1,0:T(1,128)S(1)}, u32[]{:S(2)}, u32[]{:S(2)}) collective-permute-start(s32[1,16]{1,0:T(1,128)} %bitcast.15), channel_id=1, source_target_pairs={{0,128},{32,160},{64,192},{96,224},{128,0},{160,32},{192,64},{224,... | collective-permute-start | bytes 200 | tf_op jit(solution)/shard_map/ppermute | solution.py:106
  12.0 13.9 %collective-permute-start.1 = (s32[2,16]{1,0:T(2,128)S(1)}, s32[2,16]{1,0:T(2,128)S(1)}, u32[]{:S(2)}, u32[]{:S(2)}) collective-permute-start(s32[2,16]{1,0:T(2,128)S(1)} %pad_add_fusion.2), channel_id=1, source_target_pairs={{0,256},{32,288},{64,320},{96,352},{128,384},{160,416},{192,448},{... | collective-permute-start | bytes 392 | tf_op jit(solution)/shard_map/ppermute | solution.py:106
  43.5 4.8 %collective-permute-start.5 = (s32[32,16]{1,0:T(8,128)S(1)}, s32[32,16]{1,0:T(8,128)S(1)}, u32[]{:S(2)}, u32[]{:S(2)}) collective-permute-start(s32[32,16]{1,0:T(8,128)S(1)} %concatenate.54), channel_id=1, source_target_pairs={{0,16},{8,24},{16,0},{24,8},{1,17},{9,25},{17,1},{25,9},{2,18},{10... | collective-permute-start | bytes 6152 | tf_op jit(solution)/shard_map/ppermute | solution.py:106
  53.4 5.5 %sketch.1 = (f32[264,256]{1,0:T(8,128)S(1)}, f32[264,256]{1,0:T(8,128)S(1)}, f32[264,256]{1,0:T(8,128)S(1)}, f32[264,256]{1,0:T(8,128)S(1)}) custom-call(s32[1]{0:T(128)} %bitcast.pos_ref, s32[1024,1]{1,0:T(8,128)S(1)} %reshape.39.idx_ref, s32[1,2048]{1,0:T(1,128)S(1)} %bitcast.13, f32[1,2048]{1,0:T(1,128)S(1)} %bitcast.12, f32[2048,256]{1,0:T(8,128)S(1)} %copy-done), custom_call_target="tpu_custom_call" | custom-call | tf_op jit(solution)/shard_map/sketch/pallas_call | solution.py:86
  62.2 4.5 %collective-permute-start.7 = (f32[264,256]{1,0:T(8,128)S(1)}, f32[264,256]{1,0:T(8,128)S(1)}, u32[]{:S(2)}, u32[]{:S(2)}) collective-permute-start(f32[264,256]{1,0:T(8,128)S(1)} %get-tuple-element.12), channel_id=1, source_target_pairs={{0,16},{8,24},{16,0},{24,8},{1,17},{9,25},{17,1},{25,9},{2,18},{10... | collective-permute-start | bytes 811016 | tf_op jit(solution)/shard_map/ppermute | solution.py:106
  71.6 3.6 %collective-permute-done.8 = f32[264,256]{1,0:T(8,128)S(1)} collective-permute-done((f32[264,256]{1,0:T(8,128)S(1)}, f32[264,256]{1,0:T(8,128)S(1)}, u32[]{:S(2)}, u32[]{:S(2)}) %collective-permute-start.8) | collective-permute-done | bytes 270368 | tf_op jit(solution)/shard_map/ppermute | solution.py:106
  78.6 3.4 %collective-permute-start.9 = (f32[72,256]{1,0:T(8,128)S(1)}, f32[72,256]{1,0:T(8,128)S(1)}, u32[]{:S(2)}, u32[]{:S(2)}) collective-permute-start(f32[72,256]{1,0:T(8,128)S(1)} %get-tuple-element.26), channel_id=1, source_target_pairs={{0,32},{32,0},{64,96},{96,64},{128,160},{160,128},{192,224},{224,1... | collective-permute-start | bytes 221192 | tf_op jit(solution)/shard_map/ppermute | solution.py:106
  84.6 4.2 %collective-permute-done.11 = f32[72,256]{1,0:T(8,128)S(1)} collective-permute-done((f32[72,256]{1,0:T(8,128)S(1)}, f32[72,256]{1,0:T(8,128)S(1)}, u32[]{:S(2)}, u32[]{:S(2)}) %collective-permute-start.11) | collective-permute-done | bytes 73760 | tf_op jit(solution)/shard_map/ppermute | solution.py:106
  89.0 11.2 %collective-permute-start.13 = (f32[24,256]{1,0:T(8,128)S(1)}, f32[24,256]{1,0:T(8,128)S(1)}, u32[]{:S(2)}, u32[]{:S(2)}) collective-permute-start(f32[24,256]{1,0:T(8,128)S(1)} %get-tuple-element.23), channel_id=1, source_target_pairs={{0,256},{32,288},{64,320},{96,352},{128,384},{160,416},{192,448},{... | collective-permute-start | bytes 73736 | tf_op jit(solution)/shard_map/ppermute | solution.py:106
  100.2 4.0 %collective-permute-start.12 = (f32[24,256]{1,0:T(8,128)S(1)}, f32[24,256]{1,0:T(8,128)S(1)}, u32[]{:S(2)}, u32[]{:S(2)}) collective-permute-start(f32[24,256]{1,0:T(8,128)S(1)} %get-tuple-element.24), channel_id=1, source_target_pairs={{0,128},{32,160},{64,192},{96,224},{128,0},{160,32},{192,64},{224,... | collective-permute-start | bytes 73736 | tf_op jit(solution)/shard_map/ppermute | solution.py:106
  108.6 4.3 %collective-permute-done.14 = f32[24,256]{1,0:T(8,128)S(1)} collective-permute-done((f32[24,256]{1,0:T(8,128)S(1)}, f32[24,256]{1,0:T(8,128)S(1)}, u32[]{:S(2)}, u32[]{:S(2)}) %collective-permute-start.14) | collective-permute-done | bytes 24608 | tf_op jit(solution)/shard_map/ppermute | solution.py:106
  114.9 10.0 %collective-permute-start.16 = (f32[16,256]{1,0:T(8,128)S(1)}, f32[16,256]{1,0:T(8,128)S(1)}, u32[]{:S(2)}, u32[]{:S(2)}) collective-permute-start(f32[16,256]{1,0:T(8,128)S(1)} %slice.70), channel_id=1, source_target_pairs={{0,256},{32,288},{64,320},{96,352},{128,384},{160,416},{192,448},{... | collective-permute-start | bytes 49160 | tf_op jit(solution)/shard_map/ppermute | solution.py:106
  124.9 4.3 %collective-permute-start.15 = (f32[16,256]{1,0:T(8,128)S(1)}, f32[16,256]{1,0:T(8,128)S(1)}, u32[]{:S(2)}, u32[]{:S(2)}) collective-permute-start(f32[16,256]{1,0:T(8,128)S(1)} %slice.70), channel_id=1, source_target_pairs={{0,128},{32,160},{64,192},{96,224},{128,0},{160,32},{192,64},{224,... | collective-permute-start | bytes 49160 | tf_op jit(solution)/shard_map/ppermute | solution.py:106
  129.2 4.1 %collective-permute-done.15 = f32[16,256]{1,0:T(8,128)S(1)} collective-permute-done((f32[16,256]{1,0:T(8,128)S(1)}, f32[16,256]{1,0:T(8,128)S(1)}, u32[]{:S(2)}, u32[]{:S(2)}) %collective-permute-start.15) | collective-permute-done | bytes 16416 | tf_op jit(solution)/shard_map/ppermute | solution.py:106
  133.3 3.8 %collective-permute-start.20 = (f32[64,256]{1,0:T(8,128)S(1)}, f32[64,256]{1,0:T(8,128)S(1)}, u32[]{:S(2)}, u32[]{:S(2)}) collective-permute-start(f32[64,256]{1,0:T(8,128)S(1)} %pad_maximum_fusion.3.row0), channel_id=1, source_target_pairs={{0,96},{32,64},{64,32},{96,0},{128,224},{160,192},{192,160},{224,1... | collective-permute-start | bytes 196616 | tf_op jit(solution)/shard_map/ppermute | solution.py:106
  139.0 3.5 %collective-permute-start.18 = (f32[64,256]{1,0:T(8,128)S(1)}, f32[64,256]{1,0:T(8,128)S(1)}, u32[]{:S(2)}, u32[]{:S(2)}) collective-permute-start(f32[64,256]{1,0:T(8,128)S(1)} %pad_maximum_fusion.3.row0), channel_id=1, source_target_pairs={{0,32},{32,0},{64,96},{96,64},{128,160},{160,128},{192,224},{224,1... | collective-permute-start | bytes 196616 | tf_op jit(solution)/shard_map/ppermute | solution.py:106
  152.6 3.6 %collective-permute-start.21 = (f32[384,128]{1,0:T(8,128)}, f32[384,128]{1,0:T(8,128)S(1)}, u32[]{:S(2)}, u32[]{:S(2)}) collective-permute-start(f32[384,128]{1,0:T(8,128)} %gram.1.gram0), channel_id=1, source_target_pairs={{0,8},{8,0},{16,24},{24,16},{1,9},{9,1},{17,25},{25,17},{2,10},{10... | collective-permute-start | bytes 589832 | tf_op jit(solution)/shard_map/ppermute | solution.py:106
  160.6 8.8 %factor.1 = (f32[8,2176]{1,0:T(8,128)S(1)}, f32[1,256]{1,0:T(1,128)S(1)}, f32[1,256]{1,0:T(1,128)}) custom-call(f32[384,128]{1,0:T(8,128)S(1)} %copy-done.2, f32[384,128]{1,0:T(8,128)S(1)} %collective-permute-done.21.gram1, f32[384,128]{1,0:T(8,128)S(1)} %collective-permute-done.22.gram2, f32[384,128]{1,0:T(8,128)S(1)} %collective-permute-done.23.gram3, ...), custom_call_target="tpu_custom_call" | custom-call | tf_op jit(solution)/shard_map/factor/pallas_call | solution.py:244
  169.5 26.1 %all_to_all.9 = f32[8,1,2176]{2,1,0:T(1,128)S(1)} all-to-all(f32[8,1,2176]{2,1,0:T(1,128)S(1)} %copy.20), channel_id=1, replica_groups=mesh['z'=16,'y'=4,'x'=4,'c'=2] {'x','c'}, dimensions={0} | all-to-all | bytes 139264 | tf_op jit(solution)/shard_map/all_to_all | solution.py:101
  196.9 3.7 %collective-permute-start.25 = (f32[1,128]{1,0:T(1,128)S(1)}, f32[1,128]{1,0:T(1,128)S(1)}, u32[]{:S(2)}, u32[]{:S(2)}) collective-permute-start(f32[1,128]{1,0:T(1,128)S(1)} %broadcast_in_dim.3), channel_id=1, source_target_pairs={{0,16},{8,24},{16,0},{24,8},{1,17},{9,25},{17,1},{25,9},{2,18},{10... | collective-permute-start | bytes 1544 | tf_op jit(solution)/shard_map/ppermute | solution.py:106
  200.7 4.0 %collective-permute-start.26 = (f32[1,128]{1,0:T(1,128)S(1)}, f32[1,128]{1,0:T(1,128)S(1)}, u32[]{:S(2)}, u32[]{:S(2)}) collective-permute-start(f32[1,128]{1,0:T(1,128)S(1)} %broadcast_in_dim.3), channel_id=1, source_target_pairs={{0,24},{8,16},{16,8},{24,0},{1,25},{9,17},{17,9},{25,1},{2,26},{10... | collective-permute-start | bytes 1544 | tf_op jit(solution)/shard_map/ppermute | solution.py:106
  209.7 3.4 %collective-permute-start.29 = (f32[1,128]{1,0:T(1,128)S(1)}, f32[1,128]{1,0:T(1,128)S(1)}, u32[]{:S(2)}, u32[]{:S(2)}) collective-permute-start(f32[1,128]{1,0:T(1,128)S(1)} %add_add_fusion.3), channel_id=1, source_target_pairs={{0,96},{32,64},{64,32},{96,0},{128,224},{160,192},{192,160},{224,1... | collective-permute-start | bytes 1544 | tf_op jit(solution)/shard_map/ppermute | solution.py:106
  223.6 8.6 %collective-permute-start.31 = (f32[1,128]{1,0:T(1,128)S(1)}, f32[1,128]{1,0:T(1,128)S(1)}, u32[]{:S(2)}, u32[]{:S(2)}) collective-permute-start(f32[1,128]{1,0:T(1,128)S(1)} %add_add_fusion.2), channel_id=1, source_target_pairs={{0,256},{32,288},{64,320},{96,352},{128,384},{160,416},{192,448},{... | collective-permute-start | bytes 1544 | tf_op jit(solution)/shard_map/ppermute | solution.py:106
  232.2 4.7 %collective-permute-start.30 = (f32[1,128]{1,0:T(1,128)S(1)}, f32[1,128]{1,0:T(1,128)S(1)}, u32[]{:S(2)}, u32[]{:S(2)}) collective-permute-start(f32[1,128]{1,0:T(1,128)S(1)} %add_add_fusion.2), channel_id=1, source_target_pairs={{0,128},{32,160},{64,192},{96,224},{128,0},{160,32},{192,64},{224,... | collective-permute-start | bytes 1544 | tf_op jit(solution)/shard_map/ppermute | solution.py:106
  (99 shorter events, 82.6 us)
Async XLA Ops:
  0.6 10.7 %collective-permute-start = (s32[1,16]{1,0:T(1,128)}, s32[1,16]{1,0:T(1,128)S(1)}, u32[]{:S(2)}, u32[]{:S(2)}) collective-permute-start(s32[1,16]{1,0:T(1,128)} %bitcast.15), channel_id=1, source_target_pairs={{0,128},{32,160},{64,192},{96,224},{128,0},{160,32},{192,64},{224,... | collective-permute-start | bytes 200 | tf_op jit(solution)/shard_map/ppermute | solution.py:106
  12.0 14.8 %collective-permute-start.1 = (s32[2,16]{1,0:T(2,128)S(1)}, s32[2,16]{1,0:T(2,128)S(1)}, u32[]{:S(2)}, u32[]{:S(2)}) collective-permute-start(s32[2,16]{1,0:T(2,128)S(1)} %pad_add_fusion.2), channel_id=1, source_target_pairs={{0,256},{32,288},{64,320},{96,352},{128,384},{160,416},{192,448},{... | collective-permute-start | bytes 392 | tf_op jit(solution)/shard_map/ppermute | solution.py:106
  58.9 9.8 %collective-permute-start.6 = (f32[264,256]{1,0:T(8,128)S(1)}, f32[264,256]{1,0:T(8,128)S(1)}, u32[]{:S(2)}, u32[]{:S(2)}) collective-permute-start(f32[264,256]{1,0:T(8,128)S(1)} %get-tuple-element.11), channel_id=1, source_target_pairs={{0,8},{8,0},{16,24},{24,16},{1,9},{9,1},{17,25},{25,17},{2,10},{10... | collective-permute-start | bytes 811016 | tf_op jit(solution)/shard_map/ppermute | solution.py:106
  62.2 9.3 %collective-permute-start.7 = (f32[264,256]{1,0:T(8,128)S(1)}, f32[264,256]{1,0:T(8,128)S(1)}, u32[]{:S(2)}, u32[]{:S(2)}) collective-permute-start(f32[264,256]{1,0:T(8,128)S(1)} %get-tuple-element.12), channel_id=1, source_target_pairs={{0,16},{8,24},{16,0},{24,8},{1,17},{9,25},{17,1},{25,9},{2,18},{10... | collective-permute-start | bytes 811016 | tf_op jit(solution)/shard_map/ppermute | solution.py:106
  66.8 8.4 %collective-permute-start.8 = (f32[264,256]{1,0:T(8,128)S(1)}, f32[264,256]{1,0:T(8,128)S(1)}, u32[]{:S(2)}, u32[]{:S(2)}) collective-permute-start(f32[264,256]{1,0:T(8,128)S(1)} %get-tuple-element.13), channel_id=1, source_target_pairs={{0,24},{8,16},{16,8},{24,0},{1,25},{9,17},{17,9},{25,1},{2,26},{10... | collective-permute-start | bytes 811016 | tf_op jit(solution)/shard_map/ppermute | solution.py:106
  75.3 9.3 %collective-permute-start.10 = (f32[72,256]{1,0:T(8,128)S(1)}, f32[72,256]{1,0:T(8,128)S(1)}, u32[]{:S(2)}, u32[]{:S(2)}) collective-permute-start(f32[72,256]{1,0:T(8,128)S(1)} %get-tuple-element.25), channel_id=1, source_target_pairs={{0,64},{32,96},{64,0},{96,32},{128,192},{160,224},{192,128},{224,1... | collective-permute-start | bytes 221192 | tf_op jit(solution)/shard_map/ppermute | solution.py:106
  78.6 6.0 %collective-permute-start.9 = (f32[72,256]{1,0:T(8,128)S(1)}, f32[72,256]{1,0:T(8,128)S(1)}, u32[]{:S(2)}, u32[]{:S(2)}) collective-permute-start(f32[72,256]{1,0:T(8,128)S(1)} %get-tuple-element.26), channel_id=1, source_target_pairs={{0,32},{32,0},{64,96},{96,64},{128,160},{160,128},{192,224},{224,1... | collective-permute-start | bytes 221192 | tf_op jit(solution)/shard_map/ppermute | solution.py:106
  82.0 6.9 %collective-permute-start.11 = (f32[72,256]{1,0:T(8,128)S(1)}, f32[72,256]{1,0:T(8,128)S(1)}, u32[]{:S(2)}, u32[]{:S(2)}) collective-permute-start(f32[72,256]{1,0:T(8,128)S(1)} %concatenate.65), channel_id=1, source_target_pairs={{0,96},{32,64},{64,32},{96,0},{128,224},{160,192},{192,160},{224,1... | collective-permute-start | bytes 221192 | tf_op jit(solution)/shard_map/ppermute | solution.py:106
  89.0 17.2 %collective-permute-start.13 = (f32[24,256]{1,0:T(8,128)S(1)}, f32[24,256]{1,0:T(8,128)S(1)}, u32[]{:S(2)}, u32[]{:S(2)}) collective-permute-start(f32[24,256]{1,0:T(8,128)S(1)} %get-tuple-element.23), channel_id=1, source_target_pairs={{0,256},{32,288},{64,320},{96,352},{128,384},{160,416},{192,448},{... | collective-permute-start | bytes 73736 | tf_op jit(solution)/shard_map/ppermute | solution.py:106
  100.2 8.5 %collective-permute-start.12 = (f32[24,256]{1,0:T(8,128)S(1)}, f32[24,256]{1,0:T(8,128)S(1)}, u32[]{:S(2)}, u32[]{:S(2)}) collective-permute-start(f32[24,256]{1,0:T(8,128)S(1)} %get-tuple-element.24), channel_id=1, source_target_pairs={{0,128},{32,160},{64,192},{96,224},{128,0},{160,32},{192,64},{224,... | collective-permute-start | bytes 73736 | tf_op jit(solution)/shard_map/ppermute | solution.py:106
  104.2 8.8 %collective-permute-start.14 = (f32[24,256]{1,0:T(8,128)S(1)}, f32[24,256]{1,0:T(8,128)S(1)}, u32[]{:S(2)}, u32[]{:S(2)}) collective-permute-start(f32[24,256]{1,0:T(8,128)S(1)} %concatenate.66), channel_id=1, source_target_pairs={{0,384},{32,416},{64,448},{96,480},{128,256},{160,288},{192,320},{... | collective-permute-start | bytes 73736 | tf_op jit(solution)/shard_map/ppermute | solution.py:106
  113.0 16.2 %collective-permute-start.17 = (f32[16,256]{1,0:T(8,128)S(1)}, f32[16,256]{1,0:T(8,128)S(1)}, u32[]{:S(2)}, u32[]{:S(2)}) collective-permute-start(f32[16,256]{1,0:T(8,128)S(1)} %slice.70), channel_id=1, source_target_pairs={{0,384},{32,416},{64,448},{96,480},{128,256},{160,288},{192,320},{... | collective-permute-start | bytes 49160 | tf_op jit(solution)/shard_map/ppermute | solution.py:106
  114.9 14.3 %collective-permute-start.16 = (f32[16,256]{1,0:T(8,128)S(1)}, f32[16,256]{1,0:T(8,128)S(1)}, u32[]{:S(2)}, u32[]{:S(2)}) collective-permute-start(f32[16,256]{1,0:T(8,128)S(1)} %slice.70), channel_id=1, source_target_pairs={{0,256},{32,288},{64,320},{96,352},{128,384},{160,416},{192,448},{... | collective-permute-start | bytes 49160 | tf_op jit(solution)/shard_map/ppermute | solution.py:106
  124.9 8.4 %collective-permute-start.15 = (f32[16,256]{1,0:T(8,128)S(1)}, f32[16,256]{1,0:T(8,128)S(1)}, u32[]{:S(2)}, u32[]{:S(2)}) collective-permute-start(f32[16,256]{1,0:T(8,128)S(1)} %slice.70), channel_id=1, source_target_pairs={{0,128},{32,160},{64,192},{96,224},{128,0},{160,32},{192,64},{224,... | collective-permute-start | bytes 49160 | tf_op jit(solution)/shard_map/ppermute | solution.py:106
  133.3 9.3 %collective-permute-start.20 = (f32[64,256]{1,0:T(8,128)S(1)}, f32[64,256]{1,0:T(8,128)S(1)}, u32[]{:S(2)}, u32[]{:S(2)}) collective-permute-start(f32[64,256]{1,0:T(8,128)S(1)} %pad_maximum_fusion.3.row0), channel_id=1, source_target_pairs={{0,96},{32,64},{64,32},{96,0},{128,224},{160,192},{192,160},{224,1... | collective-permute-start | bytes 196616 | tf_op jit(solution)/shard_map/ppermute | solution.py:106
  137.1 6.1 %collective-permute-start.19 = (f32[64,256]{1,0:T(8,128)S(1)}, f32[64,256]{1,0:T(8,128)S(1)}, u32[]{:S(2)}, u32[]{:S(2)}) collective-permute-start(f32[64,256]{1,0:T(8,128)S(1)} %pad_maximum_fusion.3.row0), channel_id=1, source_target_pairs={{0,64},{32,96},{64,0},{96,32},{128,192},{160,224},{192,128},{224,1... | collective-permute-start | bytes 196616 | tf_op jit(solution)/shard_map/ppermute | solution.py:106
  147.0 9.2 %collective-permute-start.23 = (f32[384,128]{1,0:T(8,128)}, f32[384,128]{1,0:T(8,128)S(1)}, u32[]{:S(2)}, u32[]{:S(2)}) collective-permute-start(f32[384,128]{1,0:T(8,128)} %gram.1.gram0), channel_id=1, source_target_pairs={{0,24},{8,16},{16,8},{24,0},{1,25},{9,17},{17,9},{25,1},{2,26},{10... | collective-permute-start | bytes 589832 | tf_op jit(solution)/shard_map/ppermute | solution.py:106
  149.6 8.1 %collective-permute-start.22 = (f32[384,128]{1,0:T(8,128)}, f32[384,128]{1,0:T(8,128)S(1)}, u32[]{:S(2)}, u32[]{:S(2)}) collective-permute-start(f32[384,128]{1,0:T(8,128)} %gram.1.gram0), channel_id=1, source_target_pairs={{0,16},{8,24},{16,0},{24,8},{1,17},{9,25},{17,1},{25,9},{2,18},{10... | collective-permute-start | bytes 589832 | tf_op jit(solution)/shard_map/ppermute | solution.py:106
  152.6 7.1 %collective-permute-start.21 = (f32[384,128]{1,0:T(8,128)}, f32[384,128]{1,0:T(8,128)S(1)}, u32[]{:S(2)}, u32[]{:S(2)}) collective-permute-start(f32[384,128]{1,0:T(8,128)} %gram.1.gram0), channel_id=1, source_target_pairs={{0,8},{8,0},{16,24},{24,16},{1,9},{9,1},{17,25},{25,17},{2,10},{10... | collective-permute-start | bytes 589832 | tf_op jit(solution)/shard_map/ppermute | solution.py:106
  196.9 9.7 %collective-permute-start.25 = (f32[1,128]{1,0:T(1,128)S(1)}, f32[1,128]{1,0:T(1,128)S(1)}, u32[]{:S(2)}, u32[]{:S(2)}) collective-permute-start(f32[1,128]{1,0:T(1,128)S(1)} %broadcast_in_dim.3), channel_id=1, source_target_pairs={{0,16},{8,24},{16,0},{24,8},{1,17},{9,25},{17,1},{25,9},{2,18},{10... | collective-permute-start | bytes 1544 | tf_op jit(solution)/shard_map/ppermute | solution.py:106
  209.7 9.3 %collective-permute-start.29 = (f32[1,128]{1,0:T(1,128)S(1)}, f32[1,128]{1,0:T(1,128)S(1)}, u32[]{:S(2)}, u32[]{:S(2)}) collective-permute-start(f32[1,128]{1,0:T(1,128)S(1)} %add_add_fusion.3), channel_id=1, source_target_pairs={{0,96},{32,64},{64,32},{96,0},{128,224},{160,192},{192,160},{224,1... | collective-permute-start | bytes 1544 | tf_op jit(solution)/shard_map/ppermute | solution.py:106
  220.7 16.7 %collective-permute-start.32 = (f32[1,128]{1,0:T(1,128)S(1)}, f32[1,128]{1,0:T(1,128)S(1)}, u32[]{:S(2)}, u32[]{:S(2)}) collective-permute-start(f32[1,128]{1,0:T(1,128)S(1)} %add_add_fusion.2), channel_id=1, source_target_pairs={{0,384},{32,416},{64,448},{96,480},{128,256},{160,288},{192,320},{... | collective-permute-start | bytes 1544 | tf_op jit(solution)/shard_map/ppermute | solution.py:106
  223.6 13.8 %collective-permute-start.31 = (f32[1,128]{1,0:T(1,128)S(1)}, f32[1,128]{1,0:T(1,128)S(1)}, u32[]{:S(2)}, u32[]{:S(2)}) collective-permute-start(f32[1,128]{1,0:T(1,128)S(1)} %add_add_fusion.2), channel_id=1, source_target_pairs={{0,256},{32,288},{64,320},{96,352},{128,384},{160,416},{192,448},{... | collective-permute-start | bytes 1544 | tf_op jit(solution)/shard_map/ppermute | solution.py:106
  232.2 8.2 %collective-permute-start.30 = (f32[1,128]{1,0:T(1,128)S(1)}, f32[1,128]{1,0:T(1,128)S(1)}, u32[]{:S(2)}, u32[]{:S(2)}) collective-permute-start(f32[1,128]{1,0:T(1,128)S(1)} %add_add_fusion.2), channel_id=1, source_target_pairs={{0,128},{32,160},{64,192},{96,224},{128,0},{160,32},{192,64},{224,... | collective-permute-start | bytes 1544 | tf_op jit(solution)/shard_map/ppermute | solution.py:106
  (20 other events, 417.5 us)
